TPU v7x, 32 devices: a whole 2x2x4 slice. The times are simulated.
32 devices in a mesh: brick: 4 (over y, x), gz: 8 (over z, core).
Axes of the slice: x: 2, y: 2, z: 4, core: 2. Of those that a mesh axis runs over, the one named last changes fastest.
Arguments:
- grad_field: float32 [5, 32, 512, 512], P(None, 'brick', 'gz'), may hold values from -3 to 3
- alpha_coef: float32 [5, 32], P(None, 'brick'), may hold values from 0.3 to 0.4
- metric_inner: float32 [32, 512], P('brick', 'gz'), may hold values from 0.5 to 2
- metric_outer: float32 [32, 512], P('brick', 'gz'), may hold values from 0.5 to 2
Outputs:
- adjoint_field: float32 [5, 32, 512, 512], P(None, 'brick', 'gz')
All inputs are finite; a program needn't handle non-finite values.
Results may differ from a plain program's by a relative error of at most 0.00012.
Values sent between devices are 32-bit elements; how exact they have to be, the bound alone decides.
A program may use at most 64 MiB of HBM per device.

v0:
```python
import jax
import jax.numpy as jnp
from jax import lax
from jax.sharding import PartitionSpec as P

smooth_weight = 0.2


def shifted(shard, axis, by):
    peers = lax.axis_size(axis)
    return lax.ppermute(shard, axis, [(i, (i + by) % peers) for i in range(peers)])


def with_halo(cells, sides, width, closed):
    for axis, dim in sides:
        count = lax.axis_size(axis)
        ends = count if closed else count - 1
        head = lax.slice_in_dim(cells, 0, width, axis=dim)
        tail = lax.slice_in_dim(cells, cells.shape[dim] - width, cells.shape[dim], axis=dim)
        cells = jnp.concatenate(
            [
                lax.ppermute(tail, axis, [(i, (i + 1) % count) for i in range(ends)]),
                cells,
                lax.ppermute(head, axis, [((i + 1) % count, i) for i in range(ends)]),
            ],
            axis=dim,
        )
    return cells


def signed_power(log_ratio, exponent):
    magnitude = jnp.exp(exponent.astype(jnp.float32) * log_ratio)
    return magnitude * (1 - 2 * (exponent % 2)).astype(jnp.float32)


def triangle_matrix(log_ratio, rows, columns):
    distance = rows[:, None] - columns[None, :]
    exponent = jnp.maximum(distance, 0)[None, None]
    powers = signed_power(log_ratio[:, :, None, None], exponent)
    return jnp.where((distance >= 0)[None, None], powers, 0.0)


def apply_triangle(matrix, values):
    return jnp.einsum("fxij,fxjy->fxiy", matrix, values, precision=lax.Precision.HIGHEST)


def sweep_ends(values, log_ratio):
    cells = values.shape[2]
    cell_index = jnp.arange(cells, dtype=jnp.int32)
    lower = triangle_matrix(log_ratio, cell_index, cell_index)
    partial_value = apply_triangle(lower, values)
    incoming = shifted(partial_value[:, :, -1, :], "gz", 1)
    entry_weight = signed_power(log_ratio[:, :, None], (cell_index + 1)[None, None, :])
    forward = partial_value + entry_weight[:, :, :, None] * incoming[:, :, None, :]
    partial_back = apply_triangle(jnp.swapaxes(lower, 2, 3), forward)
    incoming_back = shifted(partial_back[:, :, 0, :], "gz", -1)
    exit_weight = signed_power(log_ratio[:, :, None], (cells - cell_index)[None, None, :])
    return partial_back + exit_weight[:, :, :, None] * incoming_back[:, :, None, :]


def solve_cyclic(values, alpha_coef):
    ratio = 2.0 * alpha_coef / (1.0 + jnp.sqrt(1.0 - 4.0 * alpha_coef * alpha_coef))
    log_ratio = jnp.log(ratio)
    backward = sweep_ends(values, log_ratio)
    return (ratio / alpha_coef)[:, :, None, None] * backward


def stencil_apply(values, alpha_coef):
    block_cells = values.shape[2]
    near_coef = (2.0 * (alpha_coef + 2.0) / 3.0)[:, :, None, None]
    far_coef = ((4.0 * alpha_coef - 1.0) / 3.0)[:, :, None, None]
    padded = with_halo(values, (("gz", 2),), 2, True)
    up_one = padded[:, :, 3 : block_cells + 3]
    down_one = padded[:, :, 1 : block_cells + 1]
    up_two = padded[:, :, 4 : block_cells + 4]
    down_two = padded[:, :, 0:block_cells]
    return -(near_coef * (up_one - down_one) * 0.5 + far_coef * (up_two - down_two) * 0.25)


def adjoint_pass(values, alpha_coef):
    return stencil_apply(solve_cyclic(values, alpha_coef), alpha_coef)


def body(grad_field, alpha_coef, metric_inner, metric_outer):
    first = adjoint_pass(metric_inner[None, :, :, None] * grad_field, alpha_coef)
    padded = with_halo(first, (("brick", 1),), 1, False)
    smooth = first - smooth_weight * (padded[:, 2:] - 2.0 * first + padded[:, :-2])
    middle = metric_outer[None, :, :, None] * smooth
    return adjoint_pass(middle, alpha_coef)


def solution(mesh):
    placed = (P(None, "brick", "gz", None), P(None, "brick"), P("brick", "gz"), P("brick", "gz"))
    return jax.shard_map(
        body, mesh=mesh, in_specs=placed, out_specs=P(None, "brick", "gz", None), check_vma=False
    )
```

profile of v0, /device:TPU:4, one launch (start us, length us, event | category | flops | bytes accessed | tf_op | source)
XLA Modules:
  0.0 100.8 jit_solution(2428409756910929611)
XLA Ops:
  0.0 0.7 add_multiply_fusion.2
  0.7 7.7 %fusion.37 = f32[5,8,64,512]{3,2,1,0:T(8,128)S(1)} fusion(f32[5,8,64,512]{3,2,1,0:T(8,128)} %param.4, f32[8,64]{1,0:T(8,128)} %param.6, f32[64,64]{0,1:T(8,128)S(1)} %get-tuple-element.17, f32[5,8]{1,0:T(8,128)S(1)} %get-tuple-element.14, f32[64,64]{0,1:T(8,128)S(1)} %get-tuple-element.18, pred[64,64]{0,1:T(8,128)(4,1)S(1)} %fusion.71), kind=kOutput, calls=%fused_computation.51 | convolution fusion | flops 1008435200 | bytes 10524832 | tf_op jit(solution)/shard_map/fxij,fxjy->fxiy/dot_general | solution.py:44
  8.5 0.1 slice.90
  8.6 0.1 collective-permute-start
  8.7 0.1 exponential_multiply_fusion
  8.8 5.5 %collective-permute-done = f32[5,8,512]{2,1,0:T(8,128)S(1)} collective-permute-done((f32[5,8,512]{2,1,0:T(8,128)S(1)}, f32[5,8,512]{2,1,0:T(8,128)S(1)}, u32[]{:S(2)}, u32[]{:S(2)}) %collective-permute-start) | collective-permute-done | bytes 81952 | tf_op jit(solution)/shard_map/ppermute | solution.py:11
  14.3 5.6 %fusion.34 = f32[5,8,64,512]{3,2,1,0:T(8,128)S(1)} fusion(f32[5,8,64,512]{3,2,1,0:T(8,128)S(1)} %fusion.37, f32[5,8,512]{2,1,0:T(8,128)S(1)} %collective-permute-done, f32[5,8,64]{2,1,0:T(8,128)S(1)} %get-tuple-element.16, f32[64,64]{0,1:T(8,128)S(1)} %get-tuple-element.17, f32[5,8]{1,0:T(8,128)S(1)} %get-tuple-element.14, ...), kind=kOutput, calls=%fused_computation.48 | convolution fusion | flops 1009745920 | bytes 10614944 | tf_op jit(solution)/shard_map/fxij,fxjy->fxiy/dot_general | solution.py:44
  20.0 0.1 collective-permute-start.1
  20.1 2.1 %collective-permute-done.1 = f32[5,8,512]{2,1,0:T(8,128)S(1)} collective-permute-done((f32[5,8,512]{2,1,0:T(8,128)S(1)}, f32[5,8,512]{2,1,0:T(8,128)S(1)}, u32[]{:S(2)}, u32[]{:S(2)}) %collective-permute-start.1) | collective-permute-done | bytes 81952 | tf_op jit(solution)/shard_map/ppermute | solution.py:11
  22.1 1.0 add_multiply_fusion.1
  23.1 0.1 fusion.104
  23.2 3.7 %collective-permute-start.2 = (f32[5,8,2,512]{3,2,1,0:T(2,128)S(1)}, f32[5,8,2,512]{3,2,1,0:T(2,128)S(1)}, u32[]{:S(2)}, u32[]{:S(2)}) collective-permute-start(f32[5,8,2,512]{3,2,1,0:T(2,128)S(1)} %get-tuple-element.9), channel_id=1, source_target_pairs={{1,0},{2,1},{3,2},{4,3},{5,4},{6,5},{7,6},{0,7},{9,8},{10,9},{11,1... | collective-permute-start | bytes 491528 | tf_op jit(solution)/shard_map/ppermute | solution.py:24
  26.9 2.8 %collective-permute-done.2 = f32[5,8,2,512]{3,2,1,0:T(2,128)S(1)} collective-permute-done((f32[5,8,2,512]{3,2,1,0:T(2,128)S(1)}, f32[5,8,2,512]{3,2,1,0:T(2,128)S(1)}, u32[]{:S(2)}, u32[]{:S(2)}) %collective-permute-start.2) | collective-permute-done | bytes 163872 | tf_op jit(solution)/shard_map/ppermute | solution.py:24
  29.7 3.7 %collective-permute-done.3 = f32[5,8,2,512]{3,2,1,0:T(2,128)S(1)} collective-permute-done((f32[5,8,2,512]{3,2,1,0:T(2,128)S(1)}, f32[5,8,2,512]{3,2,1,0:T(2,128)S(1)}, u32[]{:S(2)}, u32[]{:S(2)}) %collective-permute-start.3) | collective-permute-done | bytes 163872 | tf_op jit(solution)/shard_map/ppermute | solution.py:22
  33.5 3.4 %fusion.12 = f32[5,8,64,512]{3,2,1,0:T(8,128)S(1)} fusion(f32[5,8,2,512]{3,2,1,0:T(2,128)S(1)} %collective-permute-done.3, f32[5,8,64,512]{3,2,1,0:T(8,128)S(1)} %add_multiply_fusion.1, f32[5,8,2,512]{3,2,1,0:T(2,128)S(1)} %collective-permute-done.2, f32[5,8]{1,0:T(8,128)S(1)} %get-tuple-element.12, f32[5,8]{1,0:T(8,128)S(1)} %get-tuple-element.11), kind=kLoop, calls=%fused_computation.20 | loop fusion | flops 15728640 | bytes 10813760 | tf_op jit(solution)/shard_map/neg | solution.py:77
  36.8 0.1 fusion.103
  36.9 3.3 %collective-permute-start.4 = (f32[5,1,64,512]{3,2,1,0:T(8,128)S(1)}, f32[5,1,64,512]{3,2,1,0:T(8,128)S(1)}, u32[]{:S(2)}, u32[]{:S(2)}) collective-permute-start(f32[5,1,64,512]{3,2,1,0:T(8,128)S(1)} %get-tuple-element.7), channel_id=1, source_target_pairs={{8,0},{16,8},{24,16},{9,1},{17,9},{25,17},{10,2},{18,10},{26,18},{... | collective-permute-start | bytes 1966088 | tf_op jit(solution)/shard_map/ppermute | solution.py:24
  40.3 2.7 %collective-permute-start.5 = (f32[5,1,64,512]{3,2,1,0:T(8,128)S(1)}, f32[5,1,64,512]{3,2,1,0:T(8,128)S(1)}, u32[]{:S(2)}, u32[]{:S(2)}) collective-permute-start(f32[5,1,64,512]{3,2,1,0:T(8,128)S(1)} %get-tuple-element.8), channel_id=1, source_target_pairs={{0,8},{8,16},{16,24},{1,9},{9,17},{17,25},{2,10},{10,18},{18,26},{... | collective-permute-start | bytes 1966088 | tf_op jit(solution)/shard_map/ppermute | solution.py:22
  43.0 12.4 %collective-permute-done.4 = f32[5,1,64,512]{3,2,1,0:T(8,128)S(1)} collective-permute-done((f32[5,1,64,512]{3,2,1,0:T(8,128)S(1)}, f32[5,1,64,512]{3,2,1,0:T(8,128)S(1)}, u32[]{:S(2)}, u32[]{:S(2)}) %collective-permute-start.4) | collective-permute-done | bytes 655392 | tf_op jit(solution)/shard_map/ppermute | solution.py:24
  55.4 8.6 %collective-permute-done.5 = f32[5,1,64,512]{3,2,1,0:T(8,128)S(1)} collective-permute-done((f32[5,1,64,512]{3,2,1,0:T(8,128)S(1)}, f32[5,1,64,512]{3,2,1,0:T(8,128)S(1)}, u32[]{:S(2)}, u32[]{:S(2)}) %collective-permute-start.5) | collective-permute-done | bytes 655392 | tf_op jit(solution)/shard_map/ppermute | solution.py:22
  64.0 6.7 %fusion.21 = f32[5,8,64,512]{3,2,1,0:T(8,128)S(1)} fusion(f32[5,8,64,512]{3,2,1,0:T(8,128)S(1)} %fusion.12, f32[5,1,64,512]{3,2,1,0:T(8,128)S(1)} %collective-permute-done.5, f32[5,1,64,512]{3,2,1,0:T(8,128)S(1)} %collective-permute-done.4, f32[8,64]{1,0:T(8,128)S(1)} %copy-done, f32[64,64]{0,1:T(8,128)S(1)} %get-tuple-element.17, ...), kind=kOutput, calls=%fused_computation.32 | convolution fusion | flops 1017610240 | bytes 11835552 | tf_op jit(solution)/shard_map/fxij,fxjy->fxiy/dot_general | solution.py:44
  70.8 0.1 slice.100
  70.9 0.1 collective-permute-start.6
  70.9 6.1 %collective-permute-done.6 = f32[5,8,512]{2,1,0:T(8,128)S(1)} collective-permute-done((f32[5,8,512]{2,1,0:T(8,128)S(1)}, f32[5,8,512]{2,1,0:T(8,128)S(1)}, u32[]{:S(2)}, u32[]{:S(2)}) %collective-permute-start.6) | collective-permute-done | bytes 81952 | tf_op jit(solution)/shard_map/ppermute | solution.py:11
  77.0 5.6 %fusion.30 = f32[5,8,64,512]{3,2,1,0:T(8,128)S(1)} fusion(f32[5,8,64,512]{3,2,1,0:T(8,128)S(1)} %fusion.21, f32[5,8,512]{2,1,0:T(8,128)S(1)} %collective-permute-done.6, f32[5,8,64]{2,1,0:T(8,128)S(1)} %get-tuple-element.16, f32[64,64]{0,1:T(8,128)S(1)} %get-tuple-element.17, f32[5,8]{1,0:T(8,128)S(1)} %get-tuple-element.14, ...), kind=kOutput, calls=%fused_computation.43 | convolution fusion | flops 1009745920 | bytes 10614944 | tf_op jit(solution)/shard_map/fxij,fxjy->fxiy/dot_general | solution.py:44
  82.8 2.1 %collective-permute-done.7 = f32[5,8,512]{2,1,0:T(8,128)S(1)} collective-permute-done((f32[5,8,512]{2,1,0:T(8,128)S(1)}, f32[5,8,512]{2,1,0:T(8,128)S(1)}, u32[]{:S(2)}, u32[]{:S(2)}) %collective-permute-start.7) | collective-permute-done | bytes 81952 | tf_op jit(solution)/shard_map/ppermute | solution.py:11
  84.9 0.9 add_multiply_fusion
  85.8 0.1 fusion.102
  86.0 3.7 %collective-permute-start.8 = (f32[5,8,2,512]{3,2,1,0:T(2,128)S(1)}, f32[5,8,2,512]{3,2,1,0:T(2,128)S(1)}, u32[]{:S(2)}, u32[]{:S(2)}) collective-permute-start(f32[5,8,2,512]{3,2,1,0:T(2,128)S(1)} %get-tuple-element.5), channel_id=1, source_target_pairs={{1,0},{2,1},{3,2},{4,3},{5,4},{6,5},{7,6},{0,7},{9,8},{10,9},{11,1... | collective-permute-start | bytes 491528 | tf_op jit(solution)/shard_map/ppermute | solution.py:24
  89.6 2.8 %collective-permute-done.8 = f32[5,8,2,512]{3,2,1,0:T(2,128)S(1)} collective-permute-done((f32[5,8,2,512]{3,2,1,0:T(2,128)S(1)}, f32[5,8,2,512]{3,2,1,0:T(2,128)S(1)}, u32[]{:S(2)}, u32[]{:S(2)}) %collective-permute-start.8) | collective-permute-done | bytes 163872 | tf_op jit(solution)/shard_map/ppermute | solution.py:24
  92.4 3.7 %collective-permute-done.9 = f32[5,8,2,512]{3,2,1,0:T(2,128)S(1)} collective-permute-done((f32[5,8,2,512]{3,2,1,0:T(2,128)S(1)}, f32[5,8,2,512]{3,2,1,0:T(2,128)S(1)}, u32[]{:S(2)}, u32[]{:S(2)}) %collective-permute-start.9) | collective-permute-done | bytes 163872 | tf_op jit(solution)/shard_map/ppermute | solution.py:22
  96.2 4.6 %fusion.5 = f32[5,8,64,512]{3,2,1,0:T(8,128)} fusion(f32[5,8,2,512]{3,2,1,0:T(2,128)S(1)} %collective-permute-done.9, f32[5,8,64,512]{3,2,1,0:T(8,128)S(1)} %add_multiply_fusion, f32[5,8,2,512]{3,2,1,0:T(2,128)S(1)} %collective-permute-done.8, f32[5,8]{1,0:T(8,128)S(1)} %get-tuple-element.12, f32[5,8]{1,0:T(8,128)S(1)} %get-tuple-element.11), kind=kLoop, calls=%fused_computation.13 | loop fusion | flops 15728640 | bytes 10813760 | tf_op jit(solution)/shard_map/neg | solution.py:77
  (15 shorter events, 0.2 us)
Async XLA Ops:
  8.6 5.7 %collective-permute-start = (f32[5,8,512]{2,1,0:T(8,128)S(1)}, f32[5,8,512]{2,1,0:T(8,128)S(1)}, u32[]{:S(2)}, u32[]{:S(2)}) collective-permute-start(f32[5,8,512]{2,1,0:T(8,128)S(1)} %bitcast.12), channel_id=1, source_target_pairs={{0,1},{1,2},{2,3},{3,4},{4,5},{5,6},{6,7},{7,0},{8,9},{9,10},{10,1... | collective-permute-start | bytes 245768 | tf_op jit(solution)/shard_map/ppermute | solution.py:11
  20.0 2.1 %collective-permute-start.1 = (f32[5,8,512]{2,1,0:T(8,128)S(1)}, f32[5,8,512]{2,1,0:T(8,128)S(1)}, u32[]{:S(2)}, u32[]{:S(2)}) collective-permute-start(f32[5,8,512]{2,1,0:T(8,128)S(1)} %bitcast.13), channel_id=1, source_target_pairs={{0,7},{1,0},{2,1},{3,2},{4,3},{5,4},{6,5},{7,6},{8,15},{9,8},{10,9... | collective-permute-start | bytes 245768 | tf_op jit(solution)/shard_map/ppermute | solution.py:11
  23.2 6.5 %collective-permute-start.2 = (f32[5,8,2,512]{3,2,1,0:T(2,128)S(1)}, f32[5,8,2,512]{3,2,1,0:T(2,128)S(1)}, u32[]{:S(2)}, u32[]{:S(2)}) collective-permute-start(f32[5,8,2,512]{3,2,1,0:T(2,128)S(1)} %get-tuple-element.9), channel_id=1, source_target_pairs={{1,0},{2,1},{3,2},{4,3},{5,4},{6,5},{7,6},{0,7},{9,8},{10,9},{11,1... | collective-permute-start | bytes 491528 | tf_op jit(solution)/shard_map/ppermute | solution.py:24
  26.9 6.5 %collective-permute-start.3 = (f32[5,8,2,512]{3,2,1,0:T(2,128)S(1)}, f32[5,8,2,512]{3,2,1,0:T(2,128)S(1)}, u32[]{:S(2)}, u32[]{:S(2)}) collective-permute-start(f32[5,8,2,512]{3,2,1,0:T(2,128)S(1)} %get-tuple-element.10), channel_id=1, source_target_pairs={{0,1},{1,2},{2,3},{3,4},{4,5},{5,6},{6,7},{7,0},{8,9},{9,10},{10,1... | collective-permute-start | bytes 491528 | tf_op jit(solution)/shard_map/ppermute | solution.py:22
  33.4 30.6 %copy-start = (f32[8,64]{1,0:T(8,128)S(1)}, f32[8,64]{1,0:T(8,128)}, u32[]{:S(2)}) copy-start(f32[8,64]{1,0:T(8,128)} %param.7) | copy-start | bytes 6148
  36.9 18.5 %collective-permute-start.4 = (f32[5,1,64,512]{3,2,1,0:T(8,128)S(1)}, f32[5,1,64,512]{3,2,1,0:T(8,128)S(1)}, u32[]{:S(2)}, u32[]{:S(2)}) collective-permute-start(f32[5,1,64,512]{3,2,1,0:T(8,128)S(1)} %get-tuple-element.7), channel_id=1, source_target_pairs={{8,0},{16,8},{24,16},{9,1},{17,9},{25,17},{10,2},{18,10},{26,18},{... | collective-permute-start | bytes 1966088 | tf_op jit(solution)/shard_map/ppermute | solution.py:24
  40.3 23.8 %collective-permute-start.5 = (f32[5,1,64,512]{3,2,1,0:T(8,128)S(1)}, f32[5,1,64,512]{3,2,1,0:T(8,128)S(1)}, u32[]{:S(2)}, u32[]{:S(2)}) collective-permute-start(f32[5,1,64,512]{3,2,1,0:T(8,128)S(1)} %get-tuple-element.8), channel_id=1, source_target_pairs={{0,8},{8,16},{16,24},{1,9},{9,17},{17,25},{2,10},{10,18},{18,26},{... | collective-permute-start | bytes 1966088 | tf_op jit(solution)/shard_map/ppermute | solution.py:22
  70.9 6.2 %collective-permute-start.6 = (f32[5,8,512]{2,1,0:T(8,128)S(1)}, f32[5,8,512]{2,1,0:T(8,128)S(1)}, u32[]{:S(2)}, u32[]{:S(2)}) collective-permute-start(f32[5,8,512]{2,1,0:T(8,128)S(1)} %bitcast.14), channel_id=1, source_target_pairs={{0,1},{1,2},{2,3},{3,4},{4,5},{5,6},{6,7},{7,0},{8,9},{9,10},{10,1... | collective-permute-start | bytes 245768 | tf_op jit(solution)/shard_map/ppermute | solution.py:11
  82.8 2.1 %collective-permute-start.7 = (f32[5,8,512]{2,1,0:T(8,128)S(1)}, f32[5,8,512]{2,1,0:T(8,128)S(1)}, u32[]{:S(2)}, u32[]{:S(2)}) collective-permute-start(f32[5,8,512]{2,1,0:T(8,128)S(1)} %bitcast.15), channel_id=1, source_target_pairs={{0,7},{1,0},{2,1},{3,2},{4,3},{5,4},{6,5},{7,6},{8,15},{9,8},{10,9... | collective-permute-start | bytes 245768 | tf_op jit(solution)/shard_map/ppermute | solution.py:11
  86.0 6.5 %collective-permute-start.8 = (f32[5,8,2,512]{3,2,1,0:T(2,128)S(1)}, f32[5,8,2,512]{3,2,1,0:T(2,128)S(1)}, u32[]{:S(2)}, u32[]{:S(2)}) collective-permute-start(f32[5,8,2,512]{3,2,1,0:T(2,128)S(1)} %get-tuple-element.5), channel_id=1, source_target_pairs={{1,0},{2,1},{3,2},{4,3},{5,4},{6,5},{7,6},{0,7},{9,8},{10,9},{11,1... | collective-permute-start | bytes 491528 | tf_op jit(solution)/shard_map/ppermute | solution.py:24
  89.6 6.5 %collective-permute-start.9 = (f32[5,8,2,512]{3,2,1,0:T(2,128)S(1)}, f32[5,8,2,512]{3,2,1,0:T(2,128)S(1)}, u32[]{:S(2)}, u32[]{:S(2)}) collective-permute-start(f32[5,8,2,512]{3,2,1,0:T(2,128)S(1)} %get-tuple-element.6), channel_id=1, source_target_pairs={{0,1},{1,2},{2,3},{3,4},{4,5},{5,6},{6,7},{7,0},{8,9},{9,10},{10,1... | collective-permute-start | bytes 491528 | tf_op jit(solution)/shard_map/ppermute | solution.py:22
where the time goes:
time: 101 us
  waiting for transfers between devices  49.9 us (49%)
  matrix products  25.7 us (25%)
  starting transfers between devices  13.6 us (13%)
  other arithmetic  10.7 us (11%)
    dot_general x4, matrix products, apply_triangle(): jnp.einsum('fxij,fxjy->fxiy', matrix, values, precision=lax.Precision.HIG...  25.7 us
    ppermute x3, waiting for transfers between devices, with_halo(): lax.ppermute(head, axis, [((i + 1) % count, i) for i in range(ends)])  18.1 us
    ppermute x3, waiting for transfers between devices, with_halo(): lax.ppermute(tail, axis, [(i, (i + 1) % count) for i in range(ends)])  16 us
    ppermute x4, waiting for transfers between devices, shifted(): lax.ppermute(shard, axis, [(i, (i + by) % peers) for i in range(peers)])  15.7 us
    ppermute x3, starting transfers between devices, with_halo(): lax.ppermute(head, axis, [((i + 1) % count, i) for i in range(ends)])  10.7 us
    neg x2, other arithmetic, stencil_apply(): -(near_coef * (up_one - down_one) * 0.5 + far_coef * (up_two - down_two)...  7.96 us
    ppermute x3, starting transfers between devices, with_halo(): lax.ppermute(tail, axis, [(i, (i + 1) % count) for i in range(ends)])  2.72 us
  transfers between devices with their start and end apart: 10, of which 10 were waited for; matrix products, arithmetic and copies ran while one was open for 0% of the time, Pallas kernels for 0%

commit v1 on v0

v1 whole, which is shorter than its diff:
```python
import functools

import jax
import jax.numpy as jnp
from jax import lax
from jax.experimental import pallas as pl
from jax.experimental.pallas import tpu as pltpu
from jax.sharding import PartitionSpec as P

smooth_weight = 0.2
MESH = pl.DeviceIdType.MESH
f32, bf16 = jnp.float32, jnp.bfloat16
LANES = 128


def line_coefs(alpha):
    ratio = 2.0 * alpha / (1.0 + jnp.sqrt(1.0 - 4.0 * alpha * alpha))
    scale = (ratio / alpha) / (1.0 - ratio * ratio)
    near = 2.0 * (alpha + 2.0) / 3.0
    far = (4.0 * alpha - 1.0) / 3.0
    p, q = -ratio, -1.0 / ratio
    amp = -scale * (near * 0.5 * (p - q) + far * 0.25 * (p * p - q * q))
    delta = scale * far * 0.25 * (p - q)
    return jnp.stack([jnp.log(ratio), amp, delta])


def parity(n):
    return 1.0 - 2.0 * lax.rem(n, 2).astype(f32)


def kernel(
    bricks, peers, g_ref, coef, metric_in, metric_out, o_ref,
    gv, ov, zs, zr, tab, etab, load_sem, out_sem, zs_sem, zr_sem, xs_sem, xr_sem,
):
    fields, lines, cells, width = ov.shape
    b, d = lax.axis_index("brick"), lax.axis_index("gz")
    right, left = lax.rem(d + 1, peers), lax.rem(d + peers - 1, peers)
    has_low, has_high = b > 0, b < bricks - 1

    def load(f):
        return pltpu.make_async_copy(g_ref.at[f], gv.at[f, pl.ds(1, lines)], load_sem.at[f])

    def store(f):
        return pltpu.make_async_copy(ov.at[f], o_ref.at[f], out_sem.at[f])

    def z_copy(ps, way, f):
        return pltpu.make_async_remote_copy(
            src_ref=zs.at[ps, way, f], dst_ref=zr.at[ps, way, f],
            send_sem=zs_sem.at[ps, way, f], recv_sem=zr_sem.at[ps, way, f],
            device_id={"gz": right if way == 0 else left}, device_id_type=MESH,
        )

    def x_copy(way, f):
        src, dst, to = (1, lines + 1, b - 1) if way == 0 else (lines, 0, b + 1)
        return pltpu.make_async_remote_copy(
            src_ref=gv.at[f, src], dst_ref=gv.at[f, dst],
            send_sem=xs_sem.at[way, f], recv_sem=xr_sem.at[way, f],
            device_id={"brick": to}, device_id_type=MESH,
        )

    for f in range(fields):
        load(f).start()

    barrier = pltpu.get_barrier_semaphore()
    for z in (left, right):
        pl.semaphore_signal(barrier, inc=1, device_id={"gz": z}, device_id_type=MESH)

    @pl.when(has_low)
    def _():
        pl.semaphore_signal(barrier, inc=1, device_id={"brick": b - 1}, device_id_type=MESH)

    @pl.when(has_high)
    def _():
        pl.semaphore_signal(barrier, inc=1, device_id={"brick": b + 1}, device_id_type=MESH)

    rows = cells + 16
    i = lax.broadcasted_iota(jnp.int32, (rows, 2 * cells), 0)
    j = lax.rem(lax.broadcasted_iota(jnp.int32, (rows, 2 * cells), 1), cells)
    n = i - j
    main = i < cells
    to_right, to_left = i == cells, i == cells + 8
    dist = jnp.where(main, jnp.abs(n), jnp.where(to_right, cells - 1 - j, j))
    side = jnp.where(n > 0, 1.0, jnp.where(n < 0, -1.0, 0.0))
    tab[0] = dist.astype(f32)
    tab[1] = jnp.where(main, side, jnp.where(to_right | to_left, 1.0, 0.0)) * parity(dist)
    tab[2] = jnp.where(main & (dist == 1), side, 0.0)
    pick = ((i == cells + 1) & (j == cells - 1)) | ((i == cells + 9) & (j == 0))
    tab[3] = jnp.where(pick, 1.0, 0.0)
    ie = lax.broadcasted_iota(jnp.int32, (cells, LANES), 0)
    etab[0] = (ie + 1).astype(f32)
    etab[1] = parity(ie + 1)
    etab[2] = (cells - ie).astype(f32)
    etab[3] = -parity(cells - ie)

    @pl.when(jnp.logical_not(has_low))
    def _():
        gv[:, 0] = jnp.zeros((fields, cells, width), f32)

    @pl.when(jnp.logical_not(has_high))
    def _():
        gv[:, lines + 1] = jnp.zeros((fields, cells, width), f32)

    pl.semaphore_wait(barrier, 2 + has_low.astype(jnp.int32) + has_high.astype(jnp.int32))

    def product(f, x, metric, values):
        log_ratio = coef[0, f, pl.ds(x, 1), :]
        amp = coef[1, f, pl.ds(x, 1), :]
        delta = coef[2, f, pl.ds(x, 1), :]
        powers = tab[1] * jnp.exp(tab[0] * log_ratio)
        mat = jnp.concatenate([powers[:cells] * amp, powers[cells:]], axis=0)
        mat = (mat + tab[2] * delta + tab[3]) * metric[pl.ds(x, 1), :]
        high = mat.astype(bf16).astype(f32)
        column = lax.broadcasted_iota(jnp.int32, mat.shape, 1)
        split = jnp.where(column < cells, high, mat - high).astype(bf16)
        vh = values.astype(bf16)
        vl = (values - vh.astype(f32)).astype(bf16)
        return jnp.dot(
            jnp.concatenate([split, split], axis=1),
            jnp.concatenate([vh, vh, vl, vl], axis=0),
            preferred_element_type=f32,
        )

    def outgoing(ps, f, x, result):
        for kind in range(2):
            zs[ps, 0, f, kind, pl.ds(x, 1), :] = result[cells + kind : cells + kind + 1]
            zs[ps, 1, f, kind, pl.ds(x, 1), :] = result[cells + 8 + kind : cells + 9 + kind]

    def inner(f, x):
        result = product(f, x, metric_in, gv[f, x + 1])
        outgoing(0, f, x, result)
        gv[f, x + 1] = result[:cells]

    def outer(f, x):
        own = gv[f, x + 1]
        smooth = own - smooth_weight * (gv[f, x + 2] - 2.0 * own + gv[f, x])
        result = product(f, x, metric_out, smooth)
        outgoing(1, f, x, result)
        ov[f, x] = result[:cells]

    def finish(ps, f, x, ref, at):
        log_ratio = coef[0, f, pl.ds(x, 1), :]
        amp = coef[1, f, pl.ds(x, 1), :]
        delta = coef[2, f, pl.ds(x, 1), :]
        from_left = amp * etab[1] * jnp.exp(etab[0] * log_ratio)
        from_right = amp * etab[3] * jnp.exp(etab[2] * log_ratio)
        ie8 = lax.broadcasted_iota(jnp.int32, (8, LANES), 0)
        first8 = jnp.where(ie8 == 0, delta, 0.0)
        last8 = jnp.where(ie8 == 7, -delta, 0.0)
        low, high, low1, high1 = (
            zr[ps, way, f, kind, pl.ds(x, 1), :] for kind in range(2) for way in range(2)
        )
        for c in range(0, width, LANES):
            cols = slice(c, c + LANES)
            value = ref[f, at, :, cols] + from_left * low[:, cols] + from_right * high[:, cols]
            head = value[:8] + first8 * low1[:, cols]
            tail = value[cells - 8 :] + last8 * high1[:, cols]
            ref[f, at, :, cols] = jnp.concatenate([head, value[8 : cells - 8], tail], axis=0)

    def loop(low, high, body, unroll):
        def step(x, _):
            body(x)
            return 0

        lax.fori_loop(low, high, step, 0, unroll=unroll)

    lag = 2

    def first_pass(t):
        @pl.when(t < fields)
        def _():
            load(t).wait()
            loop(0, lines, lambda x: inner(t, x), 4)
            z_copy(0, 0, t).start()
            z_copy(0, 1, t).start()

        @pl.when(t >= lag)
        def _():
            f = t - lag
            z_copy(0, 0, f).wait_recv()
            z_copy(0, 1, f).wait_recv()
            finish(0, f, 0, gv, 1)
            finish(0, f, lines - 1, gv, lines)

            @pl.when(has_low)
            def _():
                x_copy(0, f).start()

            @pl.when(has_high)
            def _():
                x_copy(1, f).start()

            loop(1, lines - 1, lambda x: finish(0, f, x, gv, x + 1), 3)

    loop(0, fields + lag, first_pass, 1)
    loop(0, fields, lambda f: loop(1, lines - 1, lambda x: outer(f, x), 3), 1)

    def second_pass(t):
        @pl.when(t < fields)
        def _():
            @pl.when(has_high)
            def _():
                x_copy(0, t).wait_recv()

            @pl.when(has_low)
            def _():
                x_copy(1, t).wait_recv()

            outer(t, 0)
            outer(t, lines - 1)
            z_copy(1, 0, t).start()
            z_copy(1, 1, t).start()

        @pl.when(t >= 1)
        def _():
            f = t - 1
            z_copy(1, 0, f).wait_recv()
            z_copy(1, 1, f).wait_recv()
            loop(0, lines, lambda x: finish(1, f, x, ov, x), 4)
            store(f).start()

    loop(0, fields + 1, second_pass, 1)

    def drain(f):
        store(f).wait()
        for ps in range(2):
            for way in range(2):
                z_copy(ps, way, f).wait_send()

        @pl.when(has_low)
        def _():
            x_copy(0, f).wait_send()

        @pl.when(has_high)
        def _():
            x_copy(1, f).wait_send()

    loop(0, fields, drain, 1)


def body(bricks, peers, grad_field, alpha_coef, metric_inner, metric_outer):
    fields, lines, cells, width = grad_field.shape
    coef = jnp.broadcast_to(line_coefs(alpha_coef)[..., None], (3, fields, lines, LANES))
    twice = lambda m: jnp.concatenate([m, m], axis=1)
    dma = pltpu.SemaphoreType.DMA
    vmem = pl.BlockSpec(memory_space=pltpu.VMEM)
    return pl.pallas_call(
        functools.partial(kernel, bricks, peers),
        out_shape=jax.ShapeDtypeStruct(grad_field.shape, f32),
        in_specs=[pl.BlockSpec(memory_space=pl.ANY), vmem, vmem, vmem],
        out_specs=pl.BlockSpec(memory_space=pl.ANY),
        scratch_shapes=[
            pltpu.VMEM((fields, lines + 2, cells, width), f32),
            pltpu.VMEM((fields, lines, cells, width), f32),
            pltpu.VMEM((2, 2, fields, 2, lines, width), f32),
            pltpu.VMEM((2, 2, fields, 2, lines, width), f32),
            pltpu.VMEM((4, cells + 16, 2 * cells), f32),
            pltpu.VMEM((4, cells, LANES), f32),
            dma((fields,)), dma((fields,)),
            dma((2, 2, fields)), dma((2, 2, fields)), dma((2, fields)), dma((2, fields)),
        ],
        compiler_params=pltpu.CompilerParams(
            collective_id=0, has_side_effects=True, vmem_limit_bytes=40 * 1024 * 1024
        ),
    )(grad_field, coef, twice(metric_inner), twice(metric_outer))


def solution(mesh):
    placed = (P(None, "brick", "gz", None), P(None, "brick"), P("brick", "gz"), P("brick", "gz"))
    return jax.shard_map(
        functools.partial(body, mesh.shape["brick"], mesh.shape["gz"]),
        mesh=mesh, in_specs=placed, out_specs=P(None, "brick", "gz", None), check_vma=False,
    )
```

time: 101 us -> 48.4 us (0.48)
  waiting for transfers between devices: 49.9 us -> 0 us
  Pallas kernels: 0 us -> 41.6 us
  matrix products: 25.7 us -> 0 us
  starting transfers between devices: 13.6 us -> 0 us
  other arithmetic: 10.7 us -> 1.56 us
  local copies, waits for them, and re-layouts: 0.67 us -> 4.93 us
    ppermute x10 -> x0, waiting for transfers between devices: 49.9 us -> none  [the longest x3 18.1 us: with_halo(): lax.ppermute(head, axis, [((i + 1) % count, i) for i in range(ends)])]
    pallas_call x0 -> x1, Pallas kernels: none -> 41.6 us  [body(): pl.pallas_call(functools.partial(kernel, bricks, peers), out_shape=jax.Sh...]
    dot_general x4 -> x0, matrix products: 25.7 us -> none  [apply_triangle(): jnp.einsum('fxij,fxjy->fxiy', matrix, values, precision=lax.Precision.HIG...]
    ppermute x10 -> x0, starting transfers between devices: 13.6 us -> none  [the longest x3 10.7 us: with_halo(): lax.ppermute(head, axis, [((i + 1) % count, i) for i in range(ends)])]
    neg x2 -> x0, other arithmetic: 7.96 us -> none  [stencil_apply(): -(near_coef * (up_one - down_one) * 0.5 + far_coef * (up_two - down_two)...]
    unnamed x6 -> x3, local copies, waits for them, and re-layouts: 0.03 us -> 4.85 us
    mul x3 -> x0, other arithmetic: 1.96 us -> none  [the longest x2 1.87 us: solve_cyclic(): return (ratio / alpha_coef)[:, :, None, None] * backward]
  transfers between devices with their start and end apart: 10 -> 0, of which waited for: 10 -> 0; matrix products, arithmetic and copies ran while one was open for 0% -> 0% of each run, Pallas kernels for 0% -> 0%
where the time goes in v1:
time: 48.4 us; the launch traced here: 48.2 us
  Pallas kernels  41.6 us (86%)
  local copies, waits for them, and re-layouts  4.93 us (10%)
  other arithmetic  1.56 us (3%)
    pallas_call x1, Pallas kernels, body(): pl.pallas_call(functools.partial(kernel, bricks, peers), out_shape=jax.Sh...  41.6 us
    unnamed x3, local copies, waits for them, and re-layouts  4.85 us

profile of v1, /device:TPU:4, one launch (start us, length us, event | category | flops | bytes accessed | tf_op | source)
XLA Modules:
  0.0 48.2 jit_solution(12874997994726582964)
XLA Ops:
  0.0 0.8 %pad_maximum_fusion.1 = (f32[8,128]{1,0:T(8,128)S(1)}, f32[8,128]{1,0:T(8,128)S(1)}) fusion(f32[8,64]{1,0:T(8,128)} %param.6, f32[8,64]{1,0:T(8,128)} %param.7), kind=kLoop, calls=%fused_computation.6 | loop fusion | flops 2048 | bytes 12288 | tf_op jit(solution)/shard_map/concatenate | solution.py:243
  0.8 0.7 %log_bitcast_fusion = (f32[1,5,8]{2,1,0:T(8,128)S(1)}, f32[1,5,8]{2,1,0:T(8,128)S(1)}, f32[1,5,8]{2,1,0:T(8,128)S(1)}) fusion(f32[5,8]{1,0:T(8,128)} %param.5), kind=kLoop, calls=%fused_computation.13 | loop fusion | flops 1200 | bytes 640 | tf_op jit(solution)/shard_map/stack | solution.py:24
  1.6 0.1 broadcast_in_dim.2.coef
  1.7 0.0 copy-start
  1.7 2.5 %copy-done = f32[5,8,64,512]{3,2,1,0:T(8,128)S(1)} copy-done((f32[5,8,64,512]{3,2,1,0:T(8,128)S(1)}, f32[5,8,64,512]{3,2,1,0:T(8,128)}, u32[]{:S(2)}) %copy-start) | copy-done | bytes 5242904
  4.1 41.6 %shard_map.46 = f32[5,8,64,512]{3,2,1,0:T(8,128)S(1)} custom-call(f32[5,8,64,512]{3,2,1,0:T(8,128)S(1)} %copy-done, f32[3,5,8,128]{3,2,1,0:T(8,128)S(1)} %broadcast_in_dim.2.coef, f32[8,128]{1,0:T(8,128)S(1)} %get-tuple-element.8.metric_in, f32[8,128]{1,0:T(8,128)S(1)} %get-tuple-element.9.metric_out), custom_call_target="tpu_custom_call" | custom-call | tf_op jit(solution)/shard_map/pallas_call | solution.py:246
  45.8 2.4 %copy.6 = f32[5,8,64,512]{3,2,1,0:T(8,128)} copy(f32[5,8,64,512]{3,2,1,0:T(8,128)S(1)} %shard_map.46) | data formatting | bytes 10485760
  (1 shorter events, 0.0 us)
Async XLA Ops:
  1.7 2.5 %copy-start = (f32[5,8,64,512]{3,2,1,0:T(8,128)S(1)}, f32[5,8,64,512]{3,2,1,0:T(8,128)}, u32[]{:S(2)}) copy-start(f32[5,8,64,512]{3,2,1,0:T(8,128)} %g_ref.1) | copy-start | bytes 15728644

commit v2 on v1

v2 whole, which is shorter than its diff:
```python
import functools

import jax
import jax.numpy as jnp
from jax import lax
from jax.experimental import pallas as pl
from jax.experimental.pallas import tpu as pltpu
from jax.sharding import PartitionSpec as P

smooth_weight = 0.2
MESH = pl.DeviceIdType.MESH
f32, bf16 = jnp.float32, jnp.bfloat16
LANES = 128


def line_coefs(alpha):
    ratio = 2.0 * alpha / (1.0 + jnp.sqrt(1.0 - 4.0 * alpha * alpha))
    scale = (ratio / alpha) / (1.0 - ratio * ratio)
    near = 2.0 * (alpha + 2.0) / 3.0
    far = (4.0 * alpha - 1.0) / 3.0
    p, q = -ratio, -1.0 / ratio
    amp = -scale * (near * 0.5 * (p - q) + far * 0.25 * (p * p - q * q))
    delta = scale * far * 0.25 * (p - q)
    return jnp.log(ratio), amp, delta


def parity(n):
    return 1.0 - 2.0 * lax.rem(n, 2).astype(f32)


def kernel(
    bricks, peers, g_ref, alpha_ref, metric_in_ref, metric_out_ref, o_ref,
    gv, alpha_v, metric_v, metrics, coef, rb, zs, zr, es, er, tab, etab,
    small_sem, edge_sem, load_sem, zs_sem, zr_sem, es_sem, er_sem, xs_sem, xr_sem, rs_sem, rr_sem,
):
    fields, lines, cells, width = o_ref.shape
    b, d = lax.axis_index("brick"), lax.axis_index("gz")
    right, left = lax.rem(d + 1, peers), lax.rem(d + peers - 1, peers)
    has_low, has_high = b > 0, b < bricks - 1
    odd, core = lax.rem(b, 2), lax.rem(d, 2)
    paired = bricks % 2 == 0
    toward = 1 - 2 * odd
    last = lines - 1

    def local(src, dst, sem):
        return pltpu.make_async_copy(src, dst, sem)

    small = [
        local(alpha_ref, alpha_v, small_sem.at[0]),
        local(metric_in_ref, metric_v.at[0], small_sem.at[1]),
        local(metric_out_ref, metric_v.at[1], small_sem.at[2]),
    ]
    edges = [local(g_ref.at[:, x], gv.at[:, x + 1], edge_sem.at[k]) for k, x in enumerate((0, last))]

    def load(f):
        return local(g_ref.at[f, pl.ds(1, lines - 2)], gv.at[f, pl.ds(2, lines - 2)], load_sem.at[f])

    def remote(src, dst, send_sem, recv_sem, to):
        return pltpu.make_async_remote_copy(
            src_ref=src, dst_ref=dst, send_sem=send_sem, recv_sem=recv_sem,
            device_id=to, device_id_type=MESH,
        )

    def z_copy(ps, way, f):
        to = {"gz": right if way == 0 else left}
        return remote(zs.at[ps, way, f], zr.at[ps, way, f], zs_sem.at[ps, way, f], zr_sem.at[ps, way, f], to)

    def e_copy(ps, way, f):
        to = {"gz": right if way == 0 else left}
        return remote(es.at[ps, way, f], er.at[ps, way, f], es_sem.at[ps, way, f], er_sem.at[ps, way, f], to)

    def x_copy(way, f):
        src, dst, to = (1, lines + 1, b - 1) if way == 0 else (lines, 0, b + 1)
        return remote(gv.at[f, src], gv.at[f, dst], xs_sem.at[way, f], xr_sem.at[way, f], {"brick": to})

    def pair_copy(f):
        src = jnp.where(odd == 1, 1, lines)
        dst = jnp.where(odd == 1, lines + 1, 0)
        return remote(
            gv.at[f, src], gv.at[f, dst], xs_sem.at[0, f], xr_sem.at[1 - odd, f], {"brick": b + toward}
        )

    def hop_copy(f):
        src = jnp.where(odd == 1, lines, 1)
        to = jnp.where(core == 0, b + toward, b - 2 * toward)
        return remote(gv.at[f, src], rb.at[f], xs_sem.at[1, f], rr_sem.at[f], {"brick": to})

    def relay_copy(f):
        up = jnp.where(odd == core, 1, 0)
        dst = jnp.where(up == 1, 0, lines + 1)
        to = jnp.where(core == 0, b + 2 * toward, b + toward)
        return remote(rb.at[f], gv.at[f, dst], rs_sem.at[f], xr_sem.at[up, f], {"brick": to})

    hops = ((odd == 1) & has_high) | ((odd == 0) & has_low)
    relays = (b + 2 * toward >= 0) & (b + 2 * toward < bricks)

    def send_lines(f):
        if paired:
            @pl.when(hops)
            def _():
                hop_copy(f).start()

            pair_copy(f).start()
        else:
            @pl.when(has_low)
            def _():
                x_copy(0, f).start()

            @pl.when(has_high)
            def _():
                x_copy(1, f).start()

    def relay(f):
        if paired:
            @pl.when(relays)
            def _():
                hop_copy(f).wait_recv()
                relay_copy(f).start()

    def wait_lines(f):
        @pl.when(has_high)
        def _():
            x_copy(0, f).wait_recv()

        @pl.when(has_low)
        def _():
            x_copy(1, f).wait_recv()

    def lines_sent(f):
        if paired:
            pair_copy(f).wait_send()

            @pl.when(hops)
            def _():
                hop_copy(f).wait_send()

            @pl.when(relays)
            def _():
                relay_copy(f).wait_send()
        else:
            @pl.when(has_low)
            def _():
                x_copy(0, f).wait_send()

            @pl.when(has_high)
            def _():
                x_copy(1, f).wait_send()

    barrier = pltpu.get_barrier_semaphore()
    for z in (left, right):
        pl.semaphore_signal(barrier, inc=1, device_id={"gz": z}, device_id_type=MESH)
    expected = 2
    for step in (-2, -1, 1, 2):
        there = (b + step >= 0) & (b + step < bricks)
        expected = expected + jnp.where(there, 1, 0)

        @pl.when(there)
        def _():
            pl.semaphore_signal(barrier, inc=1, device_id={"brick": b + step}, device_id_type=MESH)

    for copy in small + edges:
        copy.start()
    for f in range(fields):
        load(f).start()

    rows = cells + 16
    i = lax.broadcasted_iota(jnp.int32, (rows, 2 * cells), 0)
    j = lax.rem(lax.broadcasted_iota(jnp.int32, (rows, 2 * cells), 1), cells)
    n = i - j
    main = i < cells
    to_right, to_left = i == cells, i == cells + 8
    dist = jnp.where(main, jnp.abs(n), jnp.where(to_right, cells - 1 - j, j))
    side = jnp.where(n > 0, 1.0, jnp.where(n < 0, -1.0, 0.0))
    tab[0] = dist.astype(f32)
    tab[1] = jnp.where(main, side, jnp.where(to_right | to_left, 1.0, 0.0)) * parity(dist)
    tab[2] = jnp.where(main & (dist == 1), side, 0.0)
    pick = ((i == cells + 1) & (j == cells - 1)) | ((i == cells + 9) & (j == 0))
    tab[3] = jnp.where(pick, 1.0, 0.0)
    ie = lax.broadcasted_iota(jnp.int32, (cells, LANES), 0)
    etab[0] = (ie + 1).astype(f32)
    etab[1] = parity(ie + 1)
    etab[2] = (cells - ie).astype(f32)
    etab[3] = -parity(cells - ie)

    @pl.when(jnp.logical_not(has_low))
    def _():
        gv[:, 0] = jnp.zeros((fields, cells, width), f32)

    @pl.when(jnp.logical_not(has_high))
    def _():
        gv[:, lines + 1] = jnp.zeros((fields, cells, width), f32)

    for copy in small:
        copy.wait()
    diagonal = lax.broadcasted_iota(jnp.int32, (lines, lines), 0) == lax.broadcasted_iota(
        jnp.int32, (lines, lines), 1
    )
    for k, values in enumerate(line_coefs(alpha_v[...])):
        for f in range(fields):
            column = jnp.sum(jnp.where(diagonal, values[f : f + 1], 0.0), axis=1, keepdims=True)
            coef[k, f] = jnp.broadcast_to(column, (lines, LANES))
    for k in range(2):
        metrics[k] = jnp.concatenate([metric_v[k], metric_v[k]], axis=1)

    def line_values(f, x):
        return (coef[k, f, pl.ds(x, 1), :] for k in range(3))

    def product(ps, f, x, values):
        log_ratio, amp, delta = line_values(f, x)
        powers = tab[1] * jnp.exp(tab[0] * log_ratio)
        mat = jnp.concatenate([powers[:cells] * amp, powers[cells:]], axis=0)
        mat = (mat + tab[2] * delta + tab[3]) * metrics[ps, pl.ds(x, 1), :]
        high = mat.astype(bf16).astype(f32)
        column = lax.broadcasted_iota(jnp.int32, mat.shape, 1)
        split = jnp.where(column < cells, high, mat - high).astype(bf16)
        vh = values.astype(bf16)
        vl = (values - vh.astype(f32)).astype(bf16)
        return jnp.dot(
            jnp.concatenate([split, split], axis=1),
            jnp.concatenate([vh, vh, vl, vl], axis=0),
            preferred_element_type=f32,
        )

    def outgoing(ps, f, x, result):
        edge = isinstance(x, int)
        for kind in range(2):
            for way in range(2):
                at = cells + 8 * way + kind
                row = result[at : at + 1]
                if edge:
                    at = 2 * kind + (x > 0)
                    es[ps, way, f, at : at + 1, :] = row
                else:
                    zs[ps, way, f, kind, pl.ds(x, 1), :] = row

    def inner(f, x):
        result = product(0, f, x, gv[f, x + 1])
        outgoing(0, f, x, result)
        gv[f, x + 1] = result[:cells]

    def outer(f, x):
        own = gv[f, x + 1]
        smooth = own - smooth_weight * (gv[f, x + 2] - 2.0 * own + gv[f, x])
        result = product(1, f, x, smooth)
        outgoing(1, f, x, result)
        o_ref[f, x] = result[:cells]

    def finish(ps, f, x):
        ref, line = (gv, x + 1) if ps == 0 else (o_ref, x)
        log_ratio, amp, delta = line_values(f, x)
        from_left = amp * etab[1] * jnp.exp(etab[0] * log_ratio)
        from_right = amp * etab[3] * jnp.exp(etab[2] * log_ratio)
        ie8 = lax.broadcasted_iota(jnp.int32, (8, LANES), 0)
        first8 = jnp.where(ie8 == 0, delta, 0.0)
        last8 = jnp.where(ie8 == 7, -delta, 0.0)
        if isinstance(x, int):
            at = int(x > 0)
            low, high, low1, high1 = (
                er[ps, way, f, 2 * kind + at : 2 * kind + at + 1, :] for kind in range(2) for way in range(2)
            )
        else:
            low, high, low1, high1 = (
                zr[ps, way, f, kind, pl.ds(x, 1), :] for kind in range(2) for way in range(2)
            )
        for c in range(0, width, LANES):
            cols = slice(c, c + LANES)
            value = ref[f, line, :, cols] + from_left * low[:, cols] + from_right * high[:, cols]
            head = value[:8] + first8 * low1[:, cols]
            tail = value[cells - 8 :] + last8 * high1[:, cols]
            ref[f, line, :, cols] = jnp.concatenate([head, value[8 : cells - 8], tail], axis=0)

    def loop(low, high, body, unroll=1):
        def step(x, _):
            body(x)
            return 0

        lax.fori_loop(low, high, step, 0, unroll=unroll)

    def both(copy, ps, f, act):
        for way in range(2):
            getattr(copy(ps, way, f), act)()

    pl.semaphore_wait(barrier, expected)
    for copy in edges:
        copy.wait()

    def edges_in(f):
        inner(f, 0)
        inner(f, last)
        both(e_copy, 0, f, "start")

    def inside_in(f):
        load(f).wait()
        loop(1, last, lambda x: inner(f, x), 3)
        both(z_copy, 0, f, "start")

    def edges_first(f):
        both(e_copy, 0, f, "wait_recv")
        finish(0, f, 0)
        finish(0, f, last)
        send_lines(f)

    def inside_first(f):
        both(z_copy, 0, f, "wait_recv")
        loop(1, last, lambda x: finish(0, f, x), 3)

    def inside_out(f):
        loop(1, last, lambda x: outer(f, x), 3)
        both(z_copy, 1, f, "start")

    def inside_last(f):
        both(z_copy, 1, f, "wait_recv")
        loop(1, last, lambda x: finish(1, f, x), 3)

    loop(0, fields, edges_in)
    inside_in(0)
    loop(0, fields, edges_first)
    loop(1, fields, inside_in)
    loop(0, fields, inside_first)
    relay(0)
    loop(0, fields, inside_out)
    loop(0, fields, inside_last)

    def edges_last(t):
        @pl.when(t + 1 < fields)
        def _():
            relay(t + 1)

        @pl.when(t < fields)
        def _():
            wait_lines(t)
            outer(t, 0)
            outer(t, last)
            both(e_copy, 1, t, "start")

        @pl.when(t >= 1)
        def _():
            f = t - 1
            both(e_copy, 1, f, "wait_recv")
            finish(1, f, 0)
            finish(1, f, last)

    loop(0, fields + 1, edges_last)

    def drain(f):
        for ps in range(2):
            both(z_copy, ps, f, "wait_send")
            both(e_copy, ps, f, "wait_send")
        lines_sent(f)

    loop(0, fields, drain)


def body(bricks, peers, grad_field, alpha_coef, metric_inner, metric_outer):
    fields, lines, cells, width = grad_field.shape
    dma = pltpu.SemaphoreType.DMA
    far = pl.BlockSpec(memory_space=pltpu.HBM)
    return pl.pallas_call(
        functools.partial(kernel, bricks, peers),
        out_shape=jax.ShapeDtypeStruct(grad_field.shape, f32),
        in_specs=[far] * 4,
        out_specs=pl.BlockSpec(memory_space=pltpu.VMEM),
        scratch_shapes=[
            pltpu.VMEM((fields, lines + 2, cells, width), f32),
            pltpu.VMEM((fields, lines), f32),
            pltpu.VMEM((2, lines, cells), f32),
            pltpu.VMEM((2, lines, 2 * cells), f32),
            pltpu.VMEM((3, fields, lines, LANES), f32),
            pltpu.VMEM((fields, cells, width), f32),
            pltpu.VMEM((2, 2, fields, 2, lines, width), f32),
            pltpu.VMEM((2, 2, fields, 2, lines, width), f32),
            pltpu.VMEM((2, 2, fields, 8, width), f32),
            pltpu.VMEM((2, 2, fields, 8, width), f32),
            pltpu.VMEM((4, cells + 16, 2 * cells), f32),
            pltpu.VMEM((4, cells, LANES), f32),
            dma((3,)), dma((2,)), dma((fields,)),
            dma((2, 2, fields)), dma((2, 2, fields)), dma((2, 2, fields)), dma((2, 2, fields)),
            dma((2, fields)), dma((2, fields)), dma((fields,)), dma((fields,)),
        ],
        compiler_params=pltpu.CompilerParams(
            collective_id=0, has_side_effects=True, vmem_limit_bytes=40 * 1024 * 1024
        ),
    )(*(pltpu.with_memory_space_constraint(a, pltpu.HBM) for a in (grad_field, alpha_coef, metric_inner, metric_outer)))


def solution(mesh):
    placed = (P(None, "brick", "gz", None), P(None, "brick"), P("brick", "gz"), P("brick", "gz"))
    return jax.shard_map(
        functools.partial(body, mesh.shape["brick"], mesh.shape["gz"]),
        mesh=mesh, in_specs=placed, out_specs=P(None, "brick", "gz", None), check_vma=False,
    )
```

time: 48.4 us -> 37.9 us (0.78)
  Pallas kernels: 41.6 us -> 35.4 us
  local copies, waits for them, and re-layouts: 4.93 us -> 2.36 us
  other arithmetic: 1.56 us -> 0 us
    pallas_call x1, Pallas kernels: 41.6 us -> 35.4 us  [body(): pl.pallas_call(functools.partial(kernel, bricks, peers), out_shape=jax.Sh...]
    unnamed x3 -> x1, local copies, waits for them, and re-layouts: 4.85 us -> 2.36 us
    concatenate x1 -> x0, other arithmetic: 0.84 us -> none  [body(): twice = lambda m: jnp.concatenate([m, m], axis=1)]
    another operation x2 -> x0, other arithmetic: 0.72 us -> none  [line_coefs(): return jnp.stack([jnp.log(ratio), amp, delta])]
where the time goes in v2:
time: 37.9 us; the launch traced here: 37.7 us
  Pallas kernels  35.4 us (93%)
  local copies, waits for them, and re-layouts  2.36 us (6%)
    pallas_call x1, Pallas kernels, body(): pl.pallas_call(functools.partial(kernel, bricks, peers), out_shape=jax.Sh...  35.4 us
    unnamed x1, local copies, waits for them, and re-layouts  2.36 us

profile of v2, /device:TPU:4, one launch (start us, length us, event | category | flops | bytes accessed | tf_op | source)
XLA Modules:
  0.0 37.7 jit_solution(13772835670062263578)
XLA Ops:
  0.0 35.4 %shard_map.46 = f32[5,8,64,512]{3,2,1,0:T(8,128)S(1)} custom-call(f32[5,8,64,512]{3,2,1,0:T(8,128)} %g_ref.1, f32[5,8]{1,0:T(8,128)} %alpha_ref.1, f32[8,64]{1,0:T(8,128)} %metric_in_ref.1, f32[8,64]{1,0:T(8,128)} %metric_out_ref.1), custom_call_target="tpu_custom_call" | custom-call | tf_op jit(solution)/shard_map/pallas_call | solution.py:358
  35.4 2.4 %copy.6 = f32[5,8,64,512]{3,2,1,0:T(8,128)} copy(f32[5,8,64,512]{3,2,1,0:T(8,128)S(1)} %shard_map.46) | data formatting | bytes 10485760

commit v3 on v2

--- a/solution.py
+++ b/solution.py
@@ -29,9 +29,9 @@
 
 
 def kernel(
-    bricks, peers, g_ref, alpha_ref, metric_in_ref, metric_out_ref, o_ref,
-    gv, alpha_v, metric_v, metrics, coef, rb, zs, zr, es, er, tab, etab,
-    small_sem, edge_sem, load_sem, zs_sem, zr_sem, es_sem, er_sem, xs_sem, xr_sem, rs_sem, rr_sem,
+    bricks, peers, early, g_ref, alpha_ref, metric_in_ref, metric_out_ref, o_ref,
+    gv, alpha_v, metric_v, alpha_n, metric_n, metrics, coef, rb, zs, zr, es, er, hx, tab, etab,
+    ns_sem, nr_sem, hs_sem, hr_sem, small_sem, edge_sem, load_sem, zs_sem, zr_sem, es_sem, er_sem, xs_sem, xr_sem, rs_sem, rr_sem,
 ):
     fields, lines, cells, width = o_ref.shape
     b, d = lax.axis_index("brick"), lax.axis_index("gz")
@@ -67,23 +67,26 @@
 
     def e_copy(ps, way, f):
         to = {"gz": right if way == 0 else left}
-        return remote(es.at[ps, way, f], er.at[ps, way, f], es_sem.at[ps, way, f], er_sem.at[ps, way, f], to)
-
-    def x_copy(way, f):
-        src, dst, to = (1, lines + 1, b - 1) if way == 0 else (lines, 0, b + 1)
-        return remote(gv.at[f, src], gv.at[f, dst], xs_sem.at[way, f], xr_sem.at[way, f], {"brick": to})
-
-    def pair_copy(f):
-        src = jnp.where(odd == 1, 1, lines)
+        return remote(es.at[ps, f, :, way], er.at[ps, f, :, way], es_sem.at[ps, way, f], er_sem.at[ps, way, f], to)
+
+    def x_copy(way, f, raw=False):
+        src, dst, to = (0, lines + 1, b - 1) if way == 0 else (last, 0, b + 1)
+        return remote(line_of(f, src, raw), gv.at[f, dst], xs_sem.at[way, f], xr_sem.at[way, f], {"brick": to})
+
+    def line_of(f, index, raw):
+        return g_ref.at[f, index] if raw else gv.at[f, index + 1]
+
+    def pair_copy(f, raw=False):
+        src = line_of(f, jnp.where(odd == 1, 0, last), raw)
         dst = jnp.where(odd == 1, lines + 1, 0)
         return remote(
-            gv.at[f, src], gv.at[f, dst], xs_sem.at[0, f], xr_sem.at[1 - odd, f], {"brick": b + toward}
+            src, gv.at[f, dst], xs_sem.at[0, f], xr_sem.at[1 - odd, f], {"brick": b + toward}
         )
 
-    def hop_copy(f):
-        src = jnp.where(odd == 1, lines, 1)
+    def hop_copy(f, raw=False):
+        src = line_of(f, jnp.where(odd == 1, last, 0), raw)
         to = jnp.where(core == 0, b + toward, b - 2 * toward)
-        return remote(gv.at[f, src], rb.at[f], xs_sem.at[1, f], rr_sem.at[f], {"brick": to})
+        return remote(src, rb.at[f], xs_sem.at[1, f], rr_sem.at[f], {"brick": to})
 
     def relay_copy(f):
         up = jnp.where(odd == core, 1, 0)
@@ -94,21 +97,33 @@
     hops = ((odd == 1) & has_high) | ((odd == 0) & has_low)
     relays = (b + 2 * toward >= 0) & (b + 2 * toward < bricks)
 
-    def send_lines(f):
+    def send_lines(f, raw=False):
         if paired:
             @pl.when(hops)
             def _():
-                hop_copy(f).start()
-
-            pair_copy(f).start()
+                hop_copy(f, raw).start()
+
+            pair_copy(f, raw).start()
         else:
             @pl.when(has_low)
             def _():
-                x_copy(0, f).start()
+                x_copy(0, f, raw).start()
 
             @pl.when(has_high)
             def _():
-                x_copy(1, f).start()
+                x_copy(1, f, raw).start()
+
+    def beside(way):
+        return {"brick": b - 1 if way == 0 else b + 1}
+
+    def neighbour_copies(way):
+        return [
+            remote(src, dst.at[1 - way], ns_sem.at[way, k], nr_sem.at[way, k], beside(way))
+            for k, (src, dst) in enumerate(((alpha_ref, alpha_n), (metric_in_ref, metric_n)))
+        ]
+
+    def row_copy(way, f):
+        return remote(er.at[0, f, way], hx.at[f, 1 - way], hs_sem.at[way, f], hr_sem.at[way, f], beside(way))
 
     def relay(f):
         if paired:
@@ -162,6 +177,15 @@
         copy.start()
     for f in range(fields):
         load(f).start()
+
+    pl.semaphore_wait(barrier, expected)
+    for f in range(early):
+        send_lines(f, True)
+    for way, there in enumerate((has_low, has_high)):
+        @pl.when(there)
+        def _():
+            for copy in neighbour_copies(way):
+                copy.start()
 
     rows = cells + 16
     i = lax.broadcasted_iota(jnp.int32, (rows, 2 * cells), 0)
@@ -198,9 +222,9 @@
     for k, values in enumerate(line_coefs(alpha_v[...])):
         for f in range(fields):
             column = jnp.sum(jnp.where(diagonal, values[f : f + 1], 0.0), axis=1, keepdims=True)
-            coef[k, f] = jnp.broadcast_to(column, (lines, LANES))
+            coef[k, f, :lines] = jnp.broadcast_to(column, (lines, LANES))
     for k in range(2):
-        metrics[k] = jnp.concatenate([metric_v[k], metric_v[k]], axis=1)
+        metrics[k, :lines] = jnp.concatenate([metric_v[k], metric_v[k]], axis=1)
 
     def line_values(f, x):
         return (coef[k, f, pl.ds(x, 1), :] for k in range(3))
@@ -228,8 +252,7 @@
                 at = cells + 8 * way + kind
                 row = result[at : at + 1]
                 if edge:
-                    at = 2 * kind + (x > 0)
-                    es[ps, way, f, at : at + 1, :] = row
+                    es[ps, f, int(x > 0), way, kind : kind + 1, :] = row
                 else:
                     zs[ps, way, f, kind, pl.ds(x, 1), :] = row
 
@@ -245,8 +268,10 @@
         outgoing(1, f, x, result)
         o_ref[f, x] = result[:cells]
 
-    def finish(ps, f, x):
+    def finish(ps, f, x, halo=None):
         ref, line = (gv, x + 1) if ps == 0 else (o_ref, x)
+        if halo is not None:
+            line = halo * (lines + 1)
         log_ratio, amp, delta = line_values(f, x)
         from_left = amp * etab[1] * jnp.exp(etab[0] * log_ratio)
         from_right = amp * etab[3] * jnp.exp(etab[2] * log_ratio)
@@ -254,9 +279,9 @@
         first8 = jnp.where(ie8 == 0, delta, 0.0)
         last8 = jnp.where(ie8 == 7, -delta, 0.0)
         if isinstance(x, int):
-            at = int(x > 0)
+            rows = er.at[ps, f, int(x > 0)] if halo is None else hx.at[f, halo]
             low, high, low1, high1 = (
-                er[ps, way, f, 2 * kind + at : 2 * kind + at + 1, :] for kind in range(2) for way in range(2)
+                rows[way, kind : kind + 1, :] for kind in range(2) for way in range(2)
             )
         else:
             low, high, low1, high1 = (
@@ -280,7 +305,6 @@
         for way in range(2):
             getattr(copy(ps, way, f), act)()
 
-    pl.semaphore_wait(barrier, expected)
     for copy in edges:
         copy.wait()
 
@@ -298,7 +322,17 @@
         both(e_copy, 0, f, "wait_recv")
         finish(0, f, 0)
         finish(0, f, last)
-        send_lines(f)
+
+        @pl.when(f >= early)
+        def _():
+            send_lines(f)
+
+        @pl.when(f < early)
+        def _():
+            for way, there in enumerate((has_low, has_high)):
+                @pl.when(there)
+                def _():
+                    row_copy(way, f).start()
 
     def inside_first(f):
         both(z_copy, 0, f, "wait_recv")
@@ -321,6 +355,27 @@
     loop(0, fields, inside_out)
     loop(0, fields, inside_last)
 
+    def halo_ready(side):
+        for copy in neighbour_copies(1 - side):
+            copy.wait_recv()
+        line, row = (last, lines) if side == 0 else (0, lines + 1)
+        for k, values in enumerate(line_coefs(alpha_n[side])):
+            for f in range(early):
+                coef[k, f, row : row + 1] = jnp.broadcast_to(values[f : f + 1, line : line + 1], (1, LANES))
+        values = metric_n[side, line : line + 1, :]
+        metrics[0, row : row + 1] = jnp.concatenate([values, values], axis=1)
+
+    def halo_first(f, side):
+        row_copy(1 - side, f).wait_recv()
+        line = side * (lines + 1)
+        gv[f, line] = product(0, f, lines + side, gv[f, line])[:cells]
+        finish(0, f, lines + side, side)
+
+    for side, there in enumerate((has_low, has_high)):
+        @pl.when(there)
+        def _():
+            halo_ready(side)
+
     def edges_last(t):
         @pl.when(t + 1 < fields)
         def _():
@@ -329,6 +384,14 @@
         @pl.when(t < fields)
         def _():
             wait_lines(t)
+
+            @pl.when(t < early)
+            def _():
+                for side, there in enumerate((has_low, has_high)):
+                    @pl.when(there)
+                    def _():
+                        halo_first(t, side)
+
             outer(t, 0)
             outer(t, last)
             both(e_copy, 1, t, "start")
@@ -349,14 +412,22 @@
         lines_sent(f)
 
     loop(0, fields, drain)
+    for way, there in enumerate((has_low, has_high)):
+        @pl.when(there)
+        def _():
+            for copy in neighbour_copies(way):
+                copy.wait_send()
+            for f in range(early):
+                row_copy(way, f).wait_send()
 
 
 def body(bricks, peers, grad_field, alpha_coef, metric_inner, metric_outer):
     fields, lines, cells, width = grad_field.shape
     dma = pltpu.SemaphoreType.DMA
+    early = min(2, fields)
     far = pl.BlockSpec(memory_space=pltpu.HBM)
     return pl.pallas_call(
-        functools.partial(kernel, bricks, peers),
+        functools.partial(kernel, bricks, peers, early),
         out_shape=jax.ShapeDtypeStruct(grad_field.shape, f32),
         in_specs=[far] * 4,
         out_specs=pl.BlockSpec(memory_space=pltpu.VMEM),
@@ -364,15 +435,19 @@
             pltpu.VMEM((fields, lines + 2, cells, width), f32),
             pltpu.VMEM((fields, lines), f32),
             pltpu.VMEM((2, lines, cells), f32),
-            pltpu.VMEM((2, lines, 2 * cells), f32),
-            pltpu.VMEM((3, fields, lines, LANES), f32),
+            pltpu.VMEM((2, fields, lines), f32),
+            pltpu.VMEM((2, lines, cells), f32),
+            pltpu.VMEM((2, lines + 8, 2 * cells), f32),
+            pltpu.VMEM((3, fields, lines + 8, LANES), f32),
             pltpu.VMEM((fields, cells, width), f32),
             pltpu.VMEM((2, 2, fields, 2, lines, width), f32),
             pltpu.VMEM((2, 2, fields, 2, lines, width), f32),
-            pltpu.VMEM((2, 2, fields, 8, width), f32),
-            pltpu.VMEM((2, 2, fields, 8, width), f32),
+            pltpu.VMEM((2, fields, 2, 2, 2, width), f32),
+            pltpu.VMEM((2, fields, 2, 2, 2, width), f32),
+            pltpu.VMEM((early, 2, 2, 2, width), f32),
             pltpu.VMEM((4, cells + 16, 2 * cells), f32),
             pltpu.VMEM((4, cells, LANES), f32),
+            dma((2, 2)), dma((2, 2)), dma((2, early)), dma((2, early)),
             dma((3,)), dma((2,)), dma((fields,)),
             dma((2, 2, fields)), dma((2, 2, fields)), dma((2, 2, fields)), dma((2, 2, fields)),
             dma((2, fields)), dma((2, fields)), dma((fields,)), dma((fields,)),

time: 37.9 us -> 37.5 us (0.989)
  the two profiles are of different devices: /device:TPU:4 before, /device:TPU:2 now
where the time goes in v3:
time: 37.5 us; the launch traced here: 37.3 us
  Pallas kernels  34.9 us (93%)
  local copies, waits for them, and re-layouts  2.36 us (6%)
    pallas_call x1, Pallas kernels, body(): pl.pallas_call(functools.partial(kernel, bricks, peers, early), out_shape...  34.9 us
    unnamed x1, local copies, waits for them, and re-layouts  2.36 us

profile of v3, /device:TPU:2, one launch (start us, length us, event | category | flops | bytes accessed | tf_op | source)
XLA Modules:
  0.0 37.3 jit_solution(18046818043838393069)
XLA Ops:
  0.0 34.9 %shard_map.46 = f32[5,8,64,512]{3,2,1,0:T(8,128)S(1)} custom-call(f32[5,8,64,512]{3,2,1,0:T(8,128)} %g_ref.1, f32[5,8]{1,0:T(8,128)} %alpha_ref.1, f32[8,64]{1,0:T(8,128)} %metric_in_ref.1, f32[8,64]{1,0:T(8,128)} %metric_out_ref.1), custom_call_target="tpu_custom_call" | custom-call | tf_op jit(solution)/shard_map/pallas_call | solution.py:429
  34.9 2.4 %copy.6 = f32[5,8,64,512]{3,2,1,0:T(8,128)} copy(f32[5,8,64,512]{3,2,1,0:T(8,128)S(1)} %shard_map.46) | data formatting | bytes 10485760

commit v4 on v3

--- a/solution.py
+++ b/solution.py
@@ -30,7 +30,7 @@
 
 def kernel(
     bricks, peers, early, g_ref, alpha_ref, metric_in_ref, metric_out_ref, o_ref,
-    gv, alpha_v, metric_v, alpha_n, metric_n, metrics, coef, rb, zs, zr, es, er, hx, tab, etab,
+    gv, alpha_v, metric_v, alpha_n, metric_n, metrics, coef, rb, zs, zr, es, er, hx, tab, etab, mats, weights,
     ns_sem, nr_sem, hs_sem, hr_sem, small_sem, edge_sem, load_sem, zs_sem, zr_sem, es_sem, er_sem, xs_sem, xr_sem, rs_sem, rr_sem,
 ):
     fields, lines, cells, width = o_ref.shape
@@ -229,11 +229,17 @@
     def line_values(f, x):
         return (coef[k, f, pl.ds(x, 1), :] for k in range(3))
 
-    def product(ps, f, x, values):
-        log_ratio, amp, delta = line_values(f, x)
-        powers = tab[1] * jnp.exp(tab[0] * log_ratio)
-        mat = jnp.concatenate([powers[:cells] * amp, powers[cells:]], axis=0)
-        mat = (mat + tab[2] * delta + tab[3]) * metrics[ps, pl.ds(x, 1), :]
+    def product(ps, f, x, values, keep=True):
+        if ps == 0:
+            log_ratio, amp, delta = line_values(f, x)
+            powers = tab[1] * jnp.exp(tab[0] * log_ratio)
+            mat = jnp.concatenate([powers[:cells] * amp, powers[cells:]], axis=0)
+            mat = mat + tab[2] * delta + tab[3]
+            if keep:
+                mats[f, x] = mat
+        else:
+            mat = mats[f, x]
+        mat = mat * metrics[ps, pl.ds(x, 1), :]
         high = mat.astype(bf16).astype(f32)
         column = lax.broadcasted_iota(jnp.int32, mat.shape, 1)
         split = jnp.where(column < cells, high, mat - high).astype(bf16)
@@ -273,8 +279,14 @@
         if halo is not None:
             line = halo * (lines + 1)
         log_ratio, amp, delta = line_values(f, x)
-        from_left = amp * etab[1] * jnp.exp(etab[0] * log_ratio)
-        from_right = amp * etab[3] * jnp.exp(etab[2] * log_ratio)
+        if ps == 0:
+            from_left = amp * etab[1] * jnp.exp(etab[0] * log_ratio)
+            from_right = amp * etab[3] * jnp.exp(etab[2] * log_ratio)
+            if halo is None:
+                weights[f, x, 0] = from_left
+                weights[f, x, 1] = from_right
+        else:
+            from_left, from_right = weights[f, x, 0], weights[f, x, 1]
         ie8 = lax.broadcasted_iota(jnp.int32, (8, LANES), 0)
         first8 = jnp.where(ie8 == 0, delta, 0.0)
         last8 = jnp.where(ie8 == 7, -delta, 0.0)
@@ -315,7 +327,7 @@
 
     def inside_in(f):
         load(f).wait()
-        loop(1, last, lambda x: inner(f, x), 3)
+        loop(1, last, lambda x: inner(f, x), last - 1)
         both(z_copy, 0, f, "start")
 
     def edges_first(f):
@@ -336,24 +348,33 @@
 
     def inside_first(f):
         both(z_copy, 0, f, "wait_recv")
-        loop(1, last, lambda x: finish(0, f, x), 3)
+        loop(1, last, lambda x: finish(0, f, x), last - 1)
 
     def inside_out(f):
-        loop(1, last, lambda x: outer(f, x), 3)
+        loop(1, last, lambda x: outer(f, x), last - 1)
         both(z_copy, 1, f, "start")
 
     def inside_last(f):
         both(z_copy, 1, f, "wait_recv")
-        loop(1, last, lambda x: finish(1, f, x), 3)
+        loop(1, last, lambda x: finish(1, f, x), last - 1)
+
+    def relays_at(phase):
+        for f in range(fields):
+            if min(f, 4) == phase:
+                relay(f)
 
     loop(0, fields, edges_in)
     inside_in(0)
     loop(0, fields, edges_first)
+    relays_at(0)
     loop(1, fields, inside_in)
+    relays_at(1)
     loop(0, fields, inside_first)
-    relay(0)
+    relays_at(2)
     loop(0, fields, inside_out)
+    relays_at(3)
     loop(0, fields, inside_last)
+    relays_at(4)
 
     def halo_ready(side):
         for copy in neighbour_copies(1 - side):
@@ -368,7 +389,7 @@
     def halo_first(f, side):
         row_copy(1 - side, f).wait_recv()
         line = side * (lines + 1)
-        gv[f, line] = product(0, f, lines + side, gv[f, line])[:cells]
+        gv[f, line] = product(0, f, lines + side, gv[f, line], False)[:cells]
         finish(0, f, lines + side, side)
 
     for side, there in enumerate((has_low, has_high)):
@@ -377,10 +398,6 @@
             halo_ready(side)
 
     def edges_last(t):
-        @pl.when(t + 1 < fields)
-        def _():
-            relay(t + 1)
-
         @pl.when(t < fields)
         def _():
             wait_lines(t)
@@ -447,6 +464,8 @@
             pltpu.VMEM((early, 2, 2, 2, width), f32),
             pltpu.VMEM((4, cells + 16, 2 * cells), f32),
             pltpu.VMEM((4, cells, LANES), f32),
+            pltpu.VMEM((fields, lines, cells + 16, 2 * cells), f32),
+            pltpu.VMEM((fields, lines, 2, cells, LANES), f32),
             dma((2, 2)), dma((2, 2)), dma((2, early)), dma((2, early)),
             dma((3,)), dma((2,)), dma((fields,)),
             dma((2, 2, fields)), dma((2, 2, fields)), dma((2, 2, fields)), dma((2, 2, fields)),

time: 37.5 us -> 40.8 us (1.088)
  the two profiles are of different devices: /device:TPU:2 before, /device:TPU:0 now
where the time goes in v4:
time: 40.8 us; the launch traced here: 40.7 us
  Pallas kernels  38.3 us (94%)
  local copies, waits for them, and re-layouts  2.36 us (6%)
    pallas_call x1, Pallas kernels, body(): pl.pallas_call(functools.partial(kernel, bricks, peers, early), out_shape...  38.3 us
    unnamed x1, local copies, waits for them, and re-layouts  2.36 us

profile of v4, /device:TPU:0, one launch (start us, length us, event | category | flops | bytes accessed | tf_op | source)
XLA Modules:
  0.0 40.7 jit_solution(10130129692600207841)
XLA Ops:
  0.0 38.3 %shard_map.46 = f32[5,8,64,512]{3,2,1,0:T(8,128)S(1)} custom-call(f32[5,8,64,512]{3,2,1,0:T(8,128)} %g_ref.1, f32[5,8]{1,0:T(8,128)} %alpha_ref.1, f32[8,64]{1,0:T(8,128)} %metric_in_ref.1, f32[8,64]{1,0:T(8,128)} %metric_out_ref.1), custom_call_target="tpu_custom_call" | custom-call | tf_op jit(solution)/shard_map/pallas_call | solution.py:446
  38.3 2.4 %copy.6 = f32[5,8,64,512]{3,2,1,0:T(8,128)} copy(f32[5,8,64,512]{3,2,1,0:T(8,128)S(1)} %shard_map.46) | data formatting | bytes 10485760

commit v5 on v4

--- a/solution.py
+++ b/solution.py
@@ -83,25 +83,35 @@
             src, gv.at[f, dst], xs_sem.at[0, f], xr_sem.at[1 - odd, f], {"brick": b + toward}
         )
 
+    def far_line(f, raw):
+        return line_of(f, jnp.where(odd == 1, last, 0), raw)
+
+    def straight_copy(f, raw=False):
+        dst = jnp.where(odd == 1, 0, lines + 1)
+        return remote(
+            far_line(f, raw), gv.at[f, dst], xs_sem.at[1, f], xr_sem.at[odd, f], {"brick": b - toward}
+        )
+
     def hop_copy(f, raw=False):
-        src = line_of(f, jnp.where(odd == 1, last, 0), raw)
-        to = jnp.where(core == 0, b + toward, b - 2 * toward)
-        return remote(src, rb.at[f], xs_sem.at[1, f], rr_sem.at[f], {"brick": to})
+        return remote(far_line(f, raw), rb.at[f], xs_sem.at[1, f], rr_sem.at[f], {"brick": b - 2 * toward})
 
     def relay_copy(f):
-        up = jnp.where(odd == core, 1, 0)
-        dst = jnp.where(up == 1, 0, lines + 1)
-        to = jnp.where(core == 0, b + 2 * toward, b + toward)
-        return remote(rb.at[f], gv.at[f, dst], rs_sem.at[f], xr_sem.at[up, f], {"brick": to})
-
-    hops = ((odd == 1) & has_high) | ((odd == 0) & has_low)
-    relays = (b + 2 * toward >= 0) & (b + 2 * toward < bricks)
+        dst = jnp.where(odd == 1, 0, lines + 1)
+        return remote(rb.at[f], gv.at[f, dst], rs_sem.at[f], xr_sem.at[odd, f], {"brick": b + toward})
+
+    far = ((odd == 1) & has_high) | ((odd == 0) & has_low)
+    straight, hops = far & (core == 0), far & (core == 1)
+    relays = (b + 2 * toward >= 0) & (b + 2 * toward < bricks) & (core == 1)
 
     def send_lines(f, raw=False):
         if paired:
             @pl.when(hops)
             def _():
                 hop_copy(f, raw).start()
+
+            @pl.when(straight)
+            def _():
+                straight_copy(f, raw).start()
 
             pair_copy(f, raw).start()
         else:
@@ -145,7 +155,7 @@
         if paired:
             pair_copy(f).wait_send()
 
-            @pl.when(hops)
+            @pl.when(far)
             def _():
                 hop_copy(f).wait_send()
 
@@ -358,23 +368,15 @@
         both(z_copy, 1, f, "wait_recv")
         loop(1, last, lambda x: finish(1, f, x), last - 1)
 
-    def relays_at(phase):
-        for f in range(fields):
-            if min(f, 4) == phase:
-                relay(f)
-
     loop(0, fields, edges_in)
     inside_in(0)
     loop(0, fields, edges_first)
-    relays_at(0)
+    loop(0, early, relay)
     loop(1, fields, inside_in)
-    relays_at(1)
+    loop(early, fields, relay)
     loop(0, fields, inside_first)
-    relays_at(2)
     loop(0, fields, inside_out)
-    relays_at(3)
     loop(0, fields, inside_last)
-    relays_at(4)
 
     def halo_ready(side):
         for copy in neighbour_copies(1 - side):

time: 40.8 us -> 36.2 us (0.89)
  Pallas kernels: 38.3 us -> 33.7 us
    pallas_call x1, Pallas kernels: 38.3 us -> 33.7 us  [body(): pl.pallas_call(functools.partial(kernel, bricks, peers, early), out_shape...]
where the time goes in v5:
time: 36.2 us; the launch traced here: 36.1 us
  Pallas kernels  33.7 us (93%)
  local copies, waits for them, and re-layouts  2.36 us (7%)
    pallas_call x1, Pallas kernels, body(): pl.pallas_call(functools.partial(kernel, bricks, peers, early), out_shape...  33.7 us
    unnamed x1, local copies, waits for them, and re-layouts  2.36 us

profile of v5, /device:TPU:0, one launch (start us, length us, event | category | flops | bytes accessed | tf_op | source)
XLA Modules:
  0.0 36.1 jit_solution(4439322943379685735)
XLA Ops:
  0.0 33.7 %shard_map.46 = f32[5,8,64,512]{3,2,1,0:T(8,128)S(1)} custom-call(f32[5,8,64,512]{3,2,1,0:T(8,128)} %g_ref.1, f32[5,8]{1,0:T(8,128)} %alpha_ref.1, f32[8,64]{1,0:T(8,128)} %metric_in_ref.1, f32[8,64]{1,0:T(8,128)} %metric_out_ref.1), custom_call_target="tpu_custom_call" | custom-call | tf_op jit(solution)/shard_map/pallas_call | solution.py:448
  33.7 2.4 %copy.6 = f32[5,8,64,512]{3,2,1,0:T(8,128)} copy(f32[5,8,64,512]{3,2,1,0:T(8,128)S(1)} %shard_map.46) | data formatting | bytes 10485760

commit v6 on v5

--- a/solution.py
+++ b/solution.py
@@ -399,6 +399,8 @@
         def _():
             halo_ready(side)
 
+    lag = 3
+
     def edges_last(t):
         @pl.when(t < fields)
         def _():
@@ -415,14 +417,14 @@
             outer(t, last)
             both(e_copy, 1, t, "start")
 
-        @pl.when(t >= 1)
-        def _():
-            f = t - 1
+        @pl.when(t >= lag)
+        def _():
+            f = t - lag
             both(e_copy, 1, f, "wait_recv")
             finish(1, f, 0)
             finish(1, f, last)
 
-    loop(0, fields + 1, edges_last)
+    loop(0, fields + lag, edges_last)
 
     def drain(f):
         for ps in range(2):

time: 36.2 us -> 34.4 us (0.950)
  the two profiles are of different devices: /device:TPU:0 before, /device:TPU:1 now
where the time goes in v6:
time: 34.4 us; the launch traced here: 34.3 us
  Pallas kernels  31.9 us (93%)
  local copies, waits for them, and re-layouts  2.36 us (7%)
    pallas_call x1, Pallas kernels, body(): pl.pallas_call(functools.partial(kernel, bricks, peers, early), out_shape...  31.9 us
    unnamed x1, local copies, waits for them, and re-layouts  2.36 us

profile of v6, /device:TPU:1, one launch (start us, length us, event | category | flops | bytes accessed | tf_op | source)
XLA Modules:
  0.0 34.3 jit_solution(6748757237263695644)
XLA Ops:
  0.0 31.9 %shard_map.46 = f32[5,8,64,512]{3,2,1,0:T(8,128)S(1)} custom-call(f32[5,8,64,512]{3,2,1,0:T(8,128)} %g_ref.1, f32[5,8]{1,0:T(8,128)} %alpha_ref.1, f32[8,64]{1,0:T(8,128)} %metric_in_ref.1, f32[8,64]{1,0:T(8,128)} %metric_out_ref.1), custom_call_target="tpu_custom_call" | custom-call | tf_op jit(solution)/shard_map/pallas_call | solution.py:450
  31.9 2.4 %copy.6 = f32[5,8,64,512]{3,2,1,0:T(8,128)} copy(f32[5,8,64,512]{3,2,1,0:T(8,128)S(1)} %shard_map.46) | data formatting | bytes 10485760

commit v7 on v6

--- a/solution.py
+++ b/solution.py
@@ -376,7 +376,8 @@
     loop(early, fields, relay)
     loop(0, fields, inside_first)
     loop(0, fields, inside_out)
-    loop(0, fields, inside_last)
+    kept = min(2, fields)
+    loop(0, fields - kept, inside_last)
 
     def halo_ready(side):
         for copy in neighbour_copies(1 - side):
@@ -416,6 +417,10 @@
             outer(t, 0)
             outer(t, last)
             both(e_copy, 1, t, "start")
+
+        @pl.when((t >= fields) & (t < fields + kept))
+        def _():
+            inside_last(t - kept)
 
         @pl.when(t >= lag)
         def _():

time: 34.4 us -> 34.4 us (level)
  no operation moved by 1% of the time
where the time goes in v7:
time: 34.4 us; the launch traced here: 34.3 us
  Pallas kernels  31.9 us (93%)
  local copies, waits for them, and re-layouts  2.36 us (7%)
    pallas_call x1, Pallas kernels, body(): pl.pallas_call(functools.partial(kernel, bricks, peers, early), out_shape...  31.9 us
    unnamed x1, local copies, waits for them, and re-layouts  2.36 us

profile of v7, /device:TPU:1, one launch (start us, length us, event | category | flops | bytes accessed | tf_op | source)
XLA Modules:
  0.0 34.3 jit_solution(11550737810374808496)
XLA Ops:
  0.0 31.9 %shard_map.46 = f32[5,8,64,512]{3,2,1,0:T(8,128)S(1)} custom-call(f32[5,8,64,512]{3,2,1,0:T(8,128)} %g_ref.1, f32[5,8]{1,0:T(8,128)} %alpha_ref.1, f32[8,64]{1,0:T(8,128)} %metric_in_ref.1, f32[8,64]{1,0:T(8,128)} %metric_out_ref.1), custom_call_target="tpu_custom_call" | custom-call | tf_op jit(solution)/shard_map/pallas_call | solution.py:455
  31.9 2.4 %copy.6 = f32[5,8,64,512]{3,2,1,0:T(8,128)} copy(f32[5,8,64,512]{3,2,1,0:T(8,128)S(1)} %shard_map.46) | data formatting | bytes 10485760
